TPU v7x, 256 devices: a whole 4x4x8 slice. The times are simulated.
256 devices in a mesh: lat: 16 (over x, z_lo, core), lon: 16 (over y, z_hi).
Axes of the slice: x: 4, y: 4, z: 8 (z_hi: 4, z_lo: 2; z = z_hi * 2 + z_lo), core: 2. Of those that a mesh axis runs over, the one named last changes fastest.
Arguments:
- tracer_state: float32 [320, 1440, 128], P('lat', 'lon'), may hold values from 0.05 to 3
- limit_codes: int32 [2, 320, 1440], P(None, 'lat', 'lon'), may hold values from 0 to 4, as said below
- center_weight: float32 [320, 1440], P('lat', 'lon'), may hold values from 0.02 to 0.2
- side_weights: float32 [4, 320, 1440], P(None, 'lat', 'lon'), may hold values from 0.1 to 0.25
- growth: float32 [35], replicated, may hold values from 0.2 to 1
- half_sat: float32 [4, 35], replicated, may hold values from 0.1 to 1
- stoich: float32 [4, 35], replicated, may hold values from 0.0057142857 to 0.057142857
- mortality: float32 [35], replicated, may hold values from 0.05 to 0.3
- sinking: float32 [35], replicated, may hold values from 0.05 to 0.4
- routing: float32 [25, 35], replicated, may hold values from 0.0057142857 to 0.057142857
- remineral: float32 [25], replicated, may hold values from 0.02 to 0.3
- release: float32 [4, 25], replicated, may hold values from 0.008 to 0.08
- cotangent: float32 [320, 1440, 128], P('lat', 'lon'), may hold values from -0.5 to 1.5
Outputs:
- state_grad: float32 [320, 1440, 128], P('lat', 'lon')
- growth_grad: float32 [35], replicated
Inputs may be any that keep to these rules, and one draw needn't show every extreme that they name: `limit_codes`: 4 marks a dry cell, the same cells on every level; otherwise the code names the nutrient (0 nitrate, 1 phosphate, 2 iron, 3 silicate) that limits growth in that cell and level. The dry share differs from one device block of 20 x 90 cells to another.
All inputs are finite; a program needn't handle non-finite values.
Results may differ from a plain program's by a relative error of at most 0.0003.
Values sent between devices are 32-bit elements; how exact they have to be, the bound alone decides.
A program may use at most 64 MiB of HBM per device.

v0:
```python
import jax
import jax.numpy as jnp
from jax import lax
from jax.sharding import PartitionSpec as P

TRACERS = 64
PHYTO = 35
NUTRIENTS = 4
LEVELS = 2
SUBSTEPS = 4


def with_halo(cells, sides, width):
    for axis, dim in sides:
        count = lax.axis_size(axis)
        ends = count - 1
        head = lax.slice_in_dim(cells, 0, width, axis=dim)
        tail = lax.slice_in_dim(cells, cells.shape[dim] - width, cells.shape[dim], axis=dim)
        cells = jnp.concatenate(
            [
                lax.ppermute(tail, axis, [(i, (i + 1) % count) for i in range(ends)]),
                cells,
                lax.ppermute(head, axis, [((i + 1) % count, i) for i in range(ends)]),
            ],
            axis=dim,
        )
    return cells


def from_behind(value, axis, by):
    devices = lax.axis_size(axis)
    pairs = [(i, i + by) for i in range(devices) if 0 <= i + by < devices]
    return lax.ppermute(value, axis, pairs)


def biology(
    tracer_field,
    limit_codes,
    growth,
    half_sat,
    stoich,
    mortality,
    sinking,
    routing,
    remineral,
    release,
):
    height, breadth = (tracer_field.shape[0], tracer_field.shape[1])
    tracers = tracer_field.reshape(height, breadth, LEVELS, TRACERS)
    nutrient = tracers[..., :NUTRIENTS]
    phyto_pool = tracers[..., NUTRIENTS : NUTRIENTS + PHYTO]
    organic = tracers[..., NUTRIENTS + PHYTO :]
    chosen = (
        jnp.moveaxis(limit_codes, 0, 2)[..., None] == jnp.arange(NUTRIENTS, dtype=jnp.int32)
    ).astype(jnp.float32)
    wet_share = jnp.sum(chosen, axis=3)
    picked = jnp.sum(chosen * nutrient, axis=3)
    picked_half = jnp.einsum("hblk,kp->hblp", chosen, half_sat, precision=lax.Precision.HIGHEST)
    limitation = picked[..., None] / (
        picked[..., None] + picked_half + (1.0 - wet_share)[..., None]
    )
    light_level = 0.4 ** jnp.arange(LEVELS, dtype=jnp.float32)
    uptake = growth * light_level[:, None] * limitation * phyto_pool
    mortal_loss = mortality * phyto_pool
    grown_phyto = phyto_pool + uptake - mortal_loss
    falling = sinking * grown_phyto
    from_above = jnp.concatenate([jnp.zeros_like(falling[:, :, :1]), falling[:, :, :-1]], axis=2)
    decay_flux = remineral * organic
    nutrient_new = nutrient - jnp.einsum(
        "hblp,kp->hblk", uptake, stoich, precision=lax.Precision.HIGHEST
    )
    nutrient_new = nutrient_new + jnp.einsum(
        "hblr,kr->hblk", decay_flux, release, precision=lax.Precision.HIGHEST
    )
    organic_new = (
        organic
        + jnp.einsum("hblp,rp->hblr", mortal_loss, routing, precision=lax.Precision.HIGHEST)
        - decay_flux
    )
    outcome = jnp.concatenate(
        [nutrient_new, grown_phyto - falling + from_above, organic_new], axis=3
    )
    return outcome.reshape(height, breadth, LEVELS * TRACERS)


def advance(padded, center, sides, wet_channels):
    middle = padded[1:-1, 1:-1]
    summed = center[..., None] * middle + sides[0][..., None] * padded[1:-1, 2:]
    summed = summed + sides[1][..., None] * padded[1:-1, :-2]
    summed = (
        summed + sides[2][..., None] * padded[2:, 1:-1] + sides[3][..., None] * padded[:-2, 1:-1]
    )
    return wet_channels * summed


def retreat(bar, center, sides, wet_channels):
    gated = wet_channels * bar
    spread = jnp.pad(center[..., None] * gated, ((1, 1), (1, 1), (0, 0)))
    spread = spread + jnp.pad(sides[0][..., None] * gated, ((1, 1), (2, 0), (0, 0)))
    spread = spread + jnp.pad(sides[1][..., None] * gated, ((1, 1), (0, 2), (0, 0)))
    spread = spread + jnp.pad(sides[2][..., None] * gated, ((2, 0), (1, 1), (0, 0)))
    spread = spread + jnp.pad(sides[3][..., None] * gated, ((0, 2), (1, 1), (0, 0)))
    return spread


def extend(tracer_field, margin_width):
    return with_halo(tracer_field, (("lat", 0), ("lon", 1)), margin_width)


def along_lon(blocks, margin_width):
    core_cols = blocks.shape[1] - 2 * margin_width
    kept = blocks[:, margin_width : margin_width + core_cols]
    for offset in (1, -1):
        outgoing = (
            blocks[:, margin_width + core_cols :] if offset == 1 else blocks[:, :margin_width]
        )
        incoming = from_behind(outgoing, "lon", offset)
        if offset == 1:
            kept = kept + jnp.pad(incoming, ((0, 0), (0, core_cols - margin_width), (0, 0)))
        else:
            kept = kept + jnp.pad(incoming, ((0, 0), (core_cols - margin_width, 0), (0, 0)))
    return kept


def along_lat(blocks, margin_width):
    core_rows = blocks.shape[0] - 2 * margin_width
    kept = blocks[margin_width : margin_width + core_rows]
    for offset in (1, -1):
        outgoing = blocks[margin_width + core_rows :] if offset == 1 else blocks[:margin_width]
        incoming = from_behind(outgoing, "lat", offset)
        if offset == 1:
            kept = kept + jnp.pad(incoming, ((0, core_rows - margin_width), (0, 0), (0, 0)))
        else:
            kept = kept + jnp.pad(incoming, ((core_rows - margin_width, 0), (0, 0), (0, 0)))
    return kept


def return_margins(blocks, margin_width):
    return along_lat(along_lon(blocks, margin_width), margin_width)


def shards(
    tracer_state,
    limit_codes,
    center_weight,
    side_weights,
    growth,
    half_sat,
    stoich,
    mortality,
    sinking,
    routing,
    remineral,
    release,
    cotangent,
):
    rows_dev, cols_dev = (tracer_state.shape[0], tracer_state.shape[1])
    wet_mask = (limit_codes != 4).astype(jnp.float32)
    wet_channels = jnp.repeat(jnp.moveaxis(wet_mask, 0, 2), TRACERS, axis=2)
    masked = tracer_state * wet_channels
    moved = masked
    for step_index in range(SUBSTEPS):
        moved = advance(extend(moved, 1), center_weight, side_weights, wet_channels)

    def plain_biology(tracer_field, rates):
        return biology(
            tracer_field,
            limit_codes,
            rates,
            half_sat,
            stoich,
            mortality,
            sinking,
            routing,
            remineral,
            release,
        )

    outcome, pullback = jax.vjp(plain_biology, moved, growth)
    bar, growth_bar = pullback(cotangent)
    for step_index in range(SUBSTEPS):
        bar = return_margins(retreat(bar, center_weight, side_weights, wet_channels), 1)
    state_grad = bar * wet_channels
    cell_count = rows_dev * lax.axis_size("lat") * cols_dev * lax.axis_size("lon") * LEVELS
    growth_grad = lax.psum(growth_bar, ("lat", "lon")) / cell_count
    return (state_grad, growth_grad)


def solution(mesh):
    in_specs = (
        P("lat", "lon", None),
        P(None, "lat", "lon"),
        P("lat", "lon"),
        P(None, "lat", "lon"),
        P(),
        P(),
        P(),
        P(),
        P(),
        P(),
        P(),
        P(),
        P("lat", "lon", None),
    )
    out_specs = (P("lat", "lon", None), P())
    return jax.shard_map(shards, mesh=mesh, in_specs=in_specs, out_specs=out_specs, check_vma=False)
```

profile of v0, /device:TPU:1, one launch (start us, length us, event | category | flops | bytes accessed | tf_op | source)
XLA Modules:
  0.0 325.2 jit_solution(14538313043424869436)
XLA Ops:
  1.4 1.6 copy.27
  3.2 4.9 %collective-permute-start = (f32[1,90,128]{1,2,0:T(8,128)S(1)}, f32[1,90,128]{1,2,0:T(8,128)S(1)}, u32[]{:S(2)}, u32[]{:S(2)}) collective-permute-start(f32[1,90,128]{1,2,0:T(8,128)S(1)} %get-tuple-element.59), channel_id=1, source_target_pairs={{0,16},{16,32},{32,48},{48,64},{64,80},{80,96},{96,112},{112,128},... | collective-permute-start | bytes 138248 | tf_op jit(solution)/shard_map/ppermute | solution.py:21
  8.1 1.9 collective-permute-start.1
  10.1 3.6 %collective-permute-done.1 = f32[1,90,128]{1,2,0:T(8,128)S(1)} collective-permute-done((f32[1,90,128]{1,2,0:T(8,128)S(1)}, f32[1,90,128]{1,2,0:T(8,128)S(1)}, u32[]{:S(2)}, u32[]{:S(2)}) %collective-permute-start.1) | collective-permute-done | bytes 46112 | tf_op jit(solution)/shard_map/ppermute | solution.py:23
  13.8 1.6 fusion.73
  15.5 1.8 copy.29
  19.0 5.5 %collective-permute-start.3 = (f32[22,1,128]{2,1,0:T(1,128)S(1)}, f32[22,1,128]{2,1,0:T(1,128)S(1)}, u32[]{:S(2)}, u32[]{:S(2)}) collective-permute-start(f32[22,1,128]{2,1,0:T(1,128)S(1)} %copy.32), channel_id=1, source_target_pairs={{0,1},{1,2},{2,3},{3,4},{4,5},{5,6},{6,7},{7,8},{8,9},{9,10},{10,1... | collective-permute-start | bytes 33800 | tf_op jit(solution)/shard_map/ppermute | solution.py:21
  27.8 2.9 bitcast_multiply_fusion.8
  30.7 2.1 collective-permute-start.4
  32.9 2.2 collective-permute-start.5
  35.0 3.5 %collective-permute-done.5 = f32[1,90,128]{1,2,0:T(8,128)S(1)} collective-permute-done((f32[1,90,128]{1,2,0:T(8,128)S(1)}, f32[1,90,128]{1,2,0:T(8,128)S(1)}, u32[]{:S(2)}, u32[]{:S(2)}) %collective-permute-start.5) | collective-permute-done | bytes 46112 | tf_op jit(solution)/shard_map/ppermute | solution.py:23
  38.6 2.0 fusion.72
  40.7 1.8 copy.36
  43.8 1.8 copy.38
  45.5 6.7 %collective-permute-start.7 = (f32[22,1,128]{2,1,0:T(1,128)S(1)}, f32[22,1,128]{2,1,0:T(1,128)S(1)}, u32[]{:S(2)}, u32[]{:S(2)}) collective-permute-start(f32[22,1,128]{2,1,0:T(1,128)S(1)} %copy.38), channel_id=1, source_target_pairs={{0,1},{1,2},{2,3},{3,4},{4,5},{5,6},{6,7},{7,8},{8,9},{9,10},{10,1... | collective-permute-start | bytes 33800 | tf_op jit(solution)/shard_map/ppermute | solution.py:21
  57.2 2.9 bitcast_multiply_fusion.7
  60.2 2.1 collective-permute-start.8
  62.3 2.2 collective-permute-start.9
  64.5 3.1 convolution_add_fusion.2
  68.9 1.6 fusion.71
  70.6 1.8 copy.40
  74.1 6.4 %collective-permute-start.11 = (f32[22,1,128]{2,1,0:T(1,128)S(1)}, f32[22,1,128]{2,1,0:T(1,128)S(1)}, u32[]{:S(2)}, u32[]{:S(2)}) collective-permute-start(f32[22,1,128]{2,1,0:T(1,128)S(1)} %copy.42), channel_id=1, source_target_pairs={{0,1},{1,2},{2,3},{3,4},{4,5},{5,6},{6,7},{7,8},{8,9},{9,10},{10,1... | collective-permute-start | bytes 33800 | tf_op jit(solution)/shard_map/ppermute | solution.py:21
  80.5 2.9 fusion.45
  86.6 2.9 bitcast_multiply_fusion.6
  89.5 3.4 %collective-permute-start.12 = (f32[1,90,128]{1,2,0:T(8,128)S(1)}, f32[1,90,128]{1,2,0:T(8,128)S(1)}, u32[]{:S(2)}, u32[]{:S(2)}) collective-permute-start(f32[1,90,128]{1,2,0:T(8,128)S(1)} %get-tuple-element.53), channel_id=1, source_target_pairs={{0,16},{16,32},{32,48},{48,64},{64,80},{80,96},{96,112},{112,128},... | collective-permute-start | bytes 138248 | tf_op jit(solution)/shard_map/ppermute | solution.py:21
  93.0 2.1 collective-permute-start.13
  95.1 3.5 %collective-permute-done.13 = f32[1,90,128]{1,2,0:T(8,128)S(1)} collective-permute-done((f32[1,90,128]{1,2,0:T(8,128)S(1)}, f32[1,90,128]{1,2,0:T(8,128)S(1)}, u32[]{:S(2)}, u32[]{:S(2)}) %collective-permute-start.13) | collective-permute-done | bytes 46112 | tf_op jit(solution)/shard_map/ppermute | solution.py:23
  98.7 2.0 fusion.70
  100.7 1.8 copy.44
  103.8 1.8 copy.46
  105.6 6.4 %collective-permute-start.15 = (f32[22,1,128]{2,1,0:T(1,128)S(1)}, f32[22,1,128]{2,1,0:T(1,128)S(1)}, u32[]{:S(2)}, u32[]{:S(2)}) collective-permute-start(f32[22,1,128]{2,1,0:T(1,128)S(1)} %copy.46), channel_id=1, source_target_pairs={{0,1},{1,2},{2,3},{3,4},{4,5},{5,6},{6,7},{7,8},{8,9},{9,10},{10,1... | collective-permute-start | bytes 33800 | tf_op jit(solution)/shard_map/ppermute | solution.py:21
  115.3 3.0 bitcast_multiply_fusion.5
  123.8 1.6 fusion.69
  125.4 1.8 copy.48
  127.2 5.5 %collective-permute-start.16 = (f32[22,1,128]{2,1,0:T(1,128)S(1)}, f32[22,1,128]{2,1,0:T(1,128)S(1)}, u32[]{:S(2)}, u32[]{:S(2)}) collective-permute-start(f32[22,1,128]{2,1,0:T(1,128)S(1)} %copy.48), channel_id=1, source_target_pairs={{0,1},{1,2},{2,3},{3,4},{4,5},{5,6},{6,7},{7,8},{8,9},{9,10},{10,1... | collective-permute-start | bytes 33800 | tf_op jit(solution)/shard_map/ppermute | solution.py:33
  134.9 5.4 %collective-permute-done.17 = f32[22,1,128]{2,1,0:T(1,128)S(1)} collective-permute-done((f32[22,1,128]{2,1,0:T(1,128)S(1)}, f32[22,1,128]{2,1,0:T(1,128)S(1)}, u32[]{:S(2)}, u32[]{:S(2)}) %collective-permute-start.17) | collective-permute-done | bytes 11296 | tf_op jit(solution)/shard_map/ppermute | solution.py:33
  141.9 2.2 fusion.3
  144.1 3.3 %collective-permute-start.18 = (f32[1,90,128]{1,2,0:T(8,128)S(1)}, f32[1,90,128]{1,2,0:T(8,128)S(1)}, u32[]{:S(2)}, u32[]{:S(2)}) collective-permute-start(f32[1,90,128]{1,2,0:T(8,128)S(1)} %get-tuple-element.35), channel_id=1, source_target_pairs={{0,16},{16,32},{32,48},{48,64},{64,80},{80,96},{96,112},{112,128},... | collective-permute-start | bytes 138248 | tf_op jit(solution)/shard_map/ppermute | solution.py:33
  147.4 2.1 collective-permute-start.19
  149.6 4.1 %collective-permute-done.19 = f32[1,90,128]{1,2,0:T(8,128)S(1)} collective-permute-done((f32[1,90,128]{1,2,0:T(8,128)S(1)}, f32[1,90,128]{1,2,0:T(8,128)S(1)}, u32[]{:S(2)}, u32[]{:S(2)}) %collective-permute-start.19) | collective-permute-done | bytes 46112 | tf_op jit(solution)/shard_map/ppermute | solution.py:33
  156.0 1.6 fusion.67
  157.6 1.8 copy.52
  159.4 6.4 %collective-permute-start.20 = (f32[22,1,128]{2,1,0:T(1,128)S(1)}, f32[22,1,128]{2,1,0:T(1,128)S(1)}, u32[]{:S(2)}, u32[]{:S(2)}) collective-permute-start(f32[22,1,128]{2,1,0:T(1,128)S(1)} %copy.52), channel_id=1, source_target_pairs={{0,1},{1,2},{2,3},{3,4},{4,5},{5,6},{6,7},{7,8},{8,9},{9,10},{10,1... | collective-permute-start | bytes 33800 | tf_op jit(solution)/shard_map/ppermute | solution.py:33
  168.0 5.6 %collective-permute-done.21 = f32[22,1,128]{2,1,0:T(1,128)S(1)} collective-permute-done((f32[22,1,128]{2,1,0:T(1,128)S(1)}, f32[22,1,128]{2,1,0:T(1,128)S(1)}, u32[]{:S(2)}, u32[]{:S(2)}) %collective-permute-start.21) | collective-permute-done | bytes 11296 | tf_op jit(solution)/shard_map/ppermute | solution.py:33
  175.3 2.2 fusion.2
  177.5 3.8 %collective-permute-start.22 = (f32[1,90,128]{1,2,0:T(8,128)S(1)}, f32[1,90,128]{1,2,0:T(8,128)S(1)}, u32[]{:S(2)}, u32[]{:S(2)}) collective-permute-start(f32[1,90,128]{1,2,0:T(8,128)S(1)} %get-tuple-element.31), channel_id=1, source_target_pairs={{0,16},{16,32},{32,48},{48,64},{64,80},{80,96},{96,112},{112,128},... | collective-permute-start | bytes 138248 | tf_op jit(solution)/shard_map/ppermute | solution.py:33
  181.2 1.9 collective-permute-start.23
  183.2 4.6 %collective-permute-done.23 = f32[1,90,128]{1,2,0:T(8,128)S(1)} collective-permute-done((f32[1,90,128]{1,2,0:T(8,128)S(1)}, f32[1,90,128]{1,2,0:T(8,128)S(1)}, u32[]{:S(2)}, u32[]{:S(2)}) %collective-permute-start.23) | collective-permute-done | bytes 46112 | tf_op jit(solution)/shard_map/ppermute | solution.py:33
  190.1 1.6 fusion.65
  191.7 1.8 copy.56
  193.5 6.6 %collective-permute-start.24 = (f32[22,1,128]{2,1,0:T(1,128)S(1)}, f32[22,1,128]{2,1,0:T(1,128)S(1)}, u32[]{:S(2)}, u32[]{:S(2)}) collective-permute-start(f32[22,1,128]{2,1,0:T(1,128)S(1)} %copy.56), channel_id=1, source_target_pairs={{0,1},{1,2},{2,3},{3,4},{4,5},{5,6},{6,7},{7,8},{8,9},{9,10},{10,1... | collective-permute-start | bytes 33800 | tf_op jit(solution)/shard_map/ppermute | solution.py:33
  202.4 3.5 %collective-permute-done.25 = f32[22,1,128]{2,1,0:T(1,128)S(1)} collective-permute-done((f32[22,1,128]{2,1,0:T(1,128)S(1)}, f32[22,1,128]{2,1,0:T(1,128)S(1)}, u32[]{:S(2)}, u32[]{:S(2)}) %collective-permute-start.25) | collective-permute-done | bytes 11296 | tf_op jit(solution)/shard_map/ppermute | solution.py:33
  207.6 2.2 fusion.1
  209.8 3.3 %collective-permute-start.26 = (f32[1,90,128]{1,2,0:T(8,128)S(1)}, f32[1,90,128]{1,2,0:T(8,128)S(1)}, u32[]{:S(2)}, u32[]{:S(2)}) collective-permute-start(f32[1,90,128]{1,2,0:T(8,128)S(1)} %get-tuple-element.27), channel_id=1, source_target_pairs={{0,16},{16,32},{32,48},{48,64},{64,80},{80,96},{96,112},{112,128},... | collective-permute-start | bytes 138248 | tf_op jit(solution)/shard_map/ppermute | solution.py:33
  213.1 1.9 collective-permute-start.27
  215.0 4.6 %collective-permute-done.27 = f32[1,90,128]{1,2,0:T(8,128)S(1)} collective-permute-done((f32[1,90,128]{1,2,0:T(8,128)S(1)}, f32[1,90,128]{1,2,0:T(8,128)S(1)}, u32[]{:S(2)}, u32[]{:S(2)}) %collective-permute-start.27) | collective-permute-done | bytes 46112 | tf_op jit(solution)/shard_map/ppermute | solution.py:33
  221.9 1.6 fusion.63
  223.6 1.8 copy.60
  225.4 5.4 %collective-permute-start.28 = (f32[22,1,128]{2,1,0:T(1,128)S(1)}, f32[22,1,128]{2,1,0:T(1,128)S(1)}, u32[]{:S(2)}, u32[]{:S(2)}) collective-permute-start(f32[22,1,128]{2,1,0:T(1,128)S(1)} %copy.60), channel_id=1, source_target_pairs={{0,1},{1,2},{2,3},{3,4},{4,5},{5,6},{6,7},{7,8},{8,9},{9,10},{10,1... | collective-permute-start | bytes 33800 | tf_op jit(solution)/shard_map/ppermute | solution.py:33
  232.9 78.3 %psum.7 = f32[35]{0:T(128)S(1)} all-reduce(f32[35]{0:T(128)S(1)} %multiply_reduce_fusion.2), channel_id=1, replica_groups=mesh['lat'=16,'lon'=16] {'lat','lon'}, use_global_device_ids=true, to_apply=%region_6.0 | all-reduce | flops 35 | bytes 280 | tf_op jit(solution)/shard_map/psum | solution.py:185
  313.3 2.2 fusion
  315.5 2.6 collective-permute-start.30
  318.1 1.9 collective-permute-start.31
  320.5 3.1 collective-permute-done.31
  (127 shorter events, 53.1 us)
Async XLA Ops:
  0.6 119.2 %copy-start = (f32[25,35]{1,0:T(8,128)S(1)}, f32[25,35]{1,0:T(8,128)}, u32[]{:S(2)}) copy-start(f32[25,35]{1,0:T(8,128)} %param.22) | copy-start | bytes 10504
  3.0 7.0 %copy-start.7 = (f32[4,20,90]{2,0,1:T(4,128)S(1)}, f32[4,20,90]{2,0,1:T(4,128)}, u32[]{:S(2)}) copy-start(f32[4,20,90]{2,0,1:T(4,128)} %param.16) | copy-start | bytes 86404
  3.2 6.9 %collective-permute-start = (f32[1,90,128]{1,2,0:T(8,128)S(1)}, f32[1,90,128]{1,2,0:T(8,128)S(1)}, u32[]{:S(2)}, u32[]{:S(2)}) collective-permute-start(f32[1,90,128]{1,2,0:T(8,128)S(1)} %get-tuple-element.59), channel_id=1, source_target_pairs={{0,16},{16,32},{32,48},{48,64},{64,80},{80,96},{96,112},{112,128},... | collective-permute-start | bytes 138248 | tf_op jit(solution)/shard_map/ppermute | solution.py:21
  8.1 5.6 %collective-permute-start.1 = (f32[1,90,128]{1,2,0:T(8,128)S(1)}, f32[1,90,128]{1,2,0:T(8,128)S(1)}, u32[]{:S(2)}, u32[]{:S(2)}) collective-permute-start(f32[1,90,128]{1,2,0:T(8,128)S(1)} %get-tuple-element.58), channel_id=1, source_target_pairs={{16,0},{32,16},{48,32},{64,48},{80,64},{96,80},{112,96},{128,112},... | collective-permute-start | bytes 138248 | tf_op jit(solution)/shard_map/ppermute | solution.py:23
  17.3 7.3 %collective-permute-start.2 = (f32[22,1,128]{2,1,0:T(1,128)S(1)}, f32[22,1,128]{2,1,0:T(1,128)S(1)}, u32[]{:S(2)}, u32[]{:S(2)}) collective-permute-start(f32[22,1,128]{2,1,0:T(1,128)S(1)} %copy.29), channel_id=1, source_target_pairs={{1,0},{2,1},{3,2},{4,3},{5,4},{6,5},{7,6},{8,7},{9,8},{10,9},{11,1... | collective-permute-start | bytes 33800 | tf_op jit(solution)/shard_map/ppermute | solution.py:23
  19.0 7.2 %collective-permute-start.3 = (f32[22,1,128]{2,1,0:T(1,128)S(1)}, f32[22,1,128]{2,1,0:T(1,128)S(1)}, u32[]{:S(2)}, u32[]{:S(2)}) collective-permute-start(f32[22,1,128]{2,1,0:T(1,128)S(1)} %copy.32), channel_id=1, source_target_pairs={{0,1},{1,2},{2,3},{3,4},{4,5},{5,6},{6,7},{7,8},{8,9},{9,10},{10,1... | collective-permute-start | bytes 33800 | tf_op jit(solution)/shard_map/ppermute | solution.py:21
  24.5 3.2 copy-start.4
  30.7 4.3 %collective-permute-start.4 = (f32[1,90,128]{1,2,0:T(8,128)S(1)}, f32[1,90,128]{1,2,0:T(8,128)S(1)}, u32[]{:S(2)}, u32[]{:S(2)}) collective-permute-start(f32[1,90,128]{1,2,0:T(8,128)S(1)} %get-tuple-element.57), channel_id=1, source_target_pairs={{0,16},{16,32},{32,48},{48,64},{64,80},{80,96},{96,112},{112,128},... | collective-permute-start | bytes 138248 | tf_op jit(solution)/shard_map/ppermute | solution.py:21
  32.9 5.7 %collective-permute-start.5 = (f32[1,90,128]{1,2,0:T(8,128)S(1)}, f32[1,90,128]{1,2,0:T(8,128)S(1)}, u32[]{:S(2)}, u32[]{:S(2)}) collective-permute-start(f32[1,90,128]{1,2,0:T(8,128)S(1)} %get-tuple-element.56), channel_id=1, source_target_pairs={{16,0},{32,16},{48,32},{64,48},{80,64},{96,80},{112,96},{128,112},... | collective-permute-start | bytes 138248 | tf_op jit(solution)/shard_map/ppermute | solution.py:23
  42.5 11.5 %collective-permute-start.6 = (f32[22,1,128]{2,1,0:T(1,128)S(1)}, f32[22,1,128]{2,1,0:T(1,128)S(1)}, u32[]{:S(2)}, u32[]{:S(2)}) collective-permute-start(f32[22,1,128]{2,1,0:T(1,128)S(1)} %copy.36), channel_id=1, source_target_pairs={{1,0},{2,1},{3,2},{4,3},{5,4},{6,5},{7,6},{8,7},{9,8},{10,9},{11,1... | collective-permute-start | bytes 33800 | tf_op jit(solution)/shard_map/ppermute | solution.py:23
  45.5 10.0 %collective-permute-start.7 = (f32[22,1,128]{2,1,0:T(1,128)S(1)}, f32[22,1,128]{2,1,0:T(1,128)S(1)}, u32[]{:S(2)}, u32[]{:S(2)}) collective-permute-start(f32[22,1,128]{2,1,0:T(1,128)S(1)} %copy.38), channel_id=1, source_target_pairs={{0,1},{1,2},{2,3},{3,4},{4,5},{5,6},{6,7},{7,8},{8,9},{9,10},{10,1... | collective-permute-start | bytes 33800 | tf_op jit(solution)/shard_map/ppermute | solution.py:21
  53.9 1.7 copy-start.2
  57.2 7.3 %copy-start.9 = (f32[4,35]{1,0:T(4,128)S(1)}, f32[4,35]{1,0:T(4,128)}, u32[]{:S(2)}) copy-start(f32[4,35]{1,0:T(4,128)} %param.19) | copy-start | bytes 1684
  57.2 7.3 %copy-start.13 = (f32[35]{0:T(128)S(1)}, f32[35]{0:T(128)}, u32[]{:S(2)}) copy-start(f32[35]{0:T(128)} %param.21) | copy-start | bytes 424
  60.2 7.5 %collective-permute-start.8 = (f32[1,90,128]{1,2,0:T(8,128)S(1)}, f32[1,90,128]{1,2,0:T(8,128)S(1)}, u32[]{:S(2)}, u32[]{:S(2)}) collective-permute-start(f32[1,90,128]{1,2,0:T(8,128)S(1)} %get-tuple-element.55), channel_id=1, source_target_pairs={{0,16},{16,32},{32,48},{48,64},{64,80},{80,96},{96,112},{112,128},... | collective-permute-start | bytes 138248 | tf_op jit(solution)/shard_map/ppermute | solution.py:21
  62.3 6.5 %collective-permute-start.9 = (f32[1,90,128]{1,2,0:T(8,128)S(1)}, f32[1,90,128]{1,2,0:T(8,128)S(1)}, u32[]{:S(2)}, u32[]{:S(2)}) collective-permute-start(f32[1,90,128]{1,2,0:T(8,128)S(1)} %get-tuple-element.54), channel_id=1, source_target_pairs={{16,0},{32,16},{48,32},{64,48},{80,64},{96,80},{112,96},{128,112},... | collective-permute-start | bytes 138248 | tf_op jit(solution)/shard_map/ppermute | solution.py:23
  70.6 10.0 %copy-start.10 = (f32[4,25]{1,0:T(4,128)S(1)}, f32[4,25]{1,0:T(4,128)}, u32[]{:S(2)}) copy-start(f32[4,25]{1,0:T(4,128)} %param.24) | copy-start | bytes 1204
  70.6 10.0 %copy-start.12 = (f32[25]{0:T(128)S(1)}, f32[25]{0:T(128)}, u32[]{:S(2)}) copy-start(f32[25]{0:T(128)} %param.23) | copy-start | bytes 304
  72.4 11.0 %collective-permute-start.10 = (f32[22,1,128]{2,1,0:T(1,128)S(1)}, f32[22,1,128]{2,1,0:T(1,128)S(1)}, u32[]{:S(2)}, u32[]{:S(2)}) collective-permute-start(f32[22,1,128]{2,1,0:T(1,128)S(1)} %copy.40), channel_id=1, source_target_pairs={{1,0},{2,1},{3,2},{4,3},{5,4},{6,5},{7,6},{8,7},{9,8},{10,9},{11,1... | collective-permute-start | bytes 33800 | tf_op jit(solution)/shard_map/ppermute | solution.py:23
  74.1 10.9 %collective-permute-start.11 = (f32[22,1,128]{2,1,0:T(1,128)S(1)}, f32[22,1,128]{2,1,0:T(1,128)S(1)}, u32[]{:S(2)}, u32[]{:S(2)}) collective-permute-start(f32[22,1,128]{2,1,0:T(1,128)S(1)} %copy.42), channel_id=1, source_target_pairs={{0,1},{1,2},{2,3},{3,4},{4,5},{5,6},{6,7},{7,8},{8,9},{9,10},{10,1... | collective-permute-start | bytes 33800 | tf_op jit(solution)/shard_map/ppermute | solution.py:21
  89.5 5.6 %collective-permute-start.12 = (f32[1,90,128]{1,2,0:T(8,128)S(1)}, f32[1,90,128]{1,2,0:T(8,128)S(1)}, u32[]{:S(2)}, u32[]{:S(2)}) collective-permute-start(f32[1,90,128]{1,2,0:T(8,128)S(1)} %get-tuple-element.53), channel_id=1, source_target_pairs={{0,16},{16,32},{32,48},{48,64},{64,80},{80,96},{96,112},{112,128},... | collective-permute-start | bytes 138248 | tf_op jit(solution)/shard_map/ppermute | solution.py:21
  93.0 5.6 %collective-permute-start.13 = (f32[1,90,128]{1,2,0:T(8,128)S(1)}, f32[1,90,128]{1,2,0:T(8,128)S(1)}, u32[]{:S(2)}, u32[]{:S(2)}) collective-permute-start(f32[1,90,128]{1,2,0:T(8,128)S(1)} %get-tuple-element.52), channel_id=1, source_target_pairs={{16,0},{32,16},{48,32},{64,48},{80,64},{96,80},{112,96},{128,112},... | collective-permute-start | bytes 138248 | tf_op jit(solution)/shard_map/ppermute | solution.py:23
  100.7 11.3 %copy-start.8 = (f32[35]{0:T(128)S(1)}, f32[35]{0:T(128)}, u32[]{:S(2)}) copy-start(f32[35]{0:T(128)} %param.17) | copy-start | bytes 424
  102.5 9.6 %collective-permute-start.14 = (f32[22,1,128]{2,1,0:T(1,128)S(1)}, f32[22,1,128]{2,1,0:T(1,128)S(1)}, u32[]{:S(2)}, u32[]{:S(2)}) collective-permute-start(f32[22,1,128]{2,1,0:T(1,128)S(1)} %copy.44), channel_id=1, source_target_pairs={{1,0},{2,1},{3,2},{4,3},{5,4},{6,5},{7,6},{8,7},{9,8},{10,9},{11,1... | collective-permute-start | bytes 33800 | tf_op jit(solution)/shard_map/ppermute | solution.py:23
  105.6 8.1 %collective-permute-start.15 = (f32[22,1,128]{2,1,0:T(1,128)S(1)}, f32[22,1,128]{2,1,0:T(1,128)S(1)}, u32[]{:S(2)}, u32[]{:S(2)}) collective-permute-start(f32[22,1,128]{2,1,0:T(1,128)S(1)} %copy.46), channel_id=1, source_target_pairs={{0,1},{1,2},{2,3},{3,4},{4,5},{5,6},{6,7},{7,8},{8,9},{9,10},{10,1... | collective-permute-start | bytes 33800 | tf_op jit(solution)/shard_map/ppermute | solution.py:21
  115.3 3.0 copy-start.6
  115.3 3.2 copy-start.11
  115.3 3.2 copy-start.15
  118.5 1.3 copy-start.3
  118.5 1.4 copy-start.14
  119.9 1.3 copy-start.5
  127.2 7.2 %collective-permute-start.16 = (f32[22,1,128]{2,1,0:T(1,128)S(1)}, f32[22,1,128]{2,1,0:T(1,128)S(1)}, u32[]{:S(2)}, u32[]{:S(2)}) collective-permute-start(f32[22,1,128]{2,1,0:T(1,128)S(1)} %copy.48), channel_id=1, source_target_pairs={{0,1},{1,2},{2,3},{3,4},{4,5},{5,6},{6,7},{7,8},{8,9},{9,10},{10,1... | collective-permute-start | bytes 33800 | tf_op jit(solution)/shard_map/ppermute | solution.py:33
  133.1 7.1 %collective-permute-start.17 = (f32[22,1,128]{2,1,0:T(1,128)S(1)}, f32[22,1,128]{2,1,0:T(1,128)S(1)}, u32[]{:S(2)}, u32[]{:S(2)}) collective-permute-start(f32[22,1,128]{2,1,0:T(1,128)S(1)} %copy.50), channel_id=1, source_target_pairs={{1,0},{2,1},{3,2},{4,3},{5,4},{6,5},{7,6},{8,7},{9,8},{10,9},{11,1... | collective-permute-start | bytes 33800 | tf_op jit(solution)/shard_map/ppermute | solution.py:33
  144.1 5.5 %collective-permute-start.18 = (f32[1,90,128]{1,2,0:T(8,128)S(1)}, f32[1,90,128]{1,2,0:T(8,128)S(1)}, u32[]{:S(2)}, u32[]{:S(2)}) collective-permute-start(f32[1,90,128]{1,2,0:T(8,128)S(1)} %get-tuple-element.35), channel_id=1, source_target_pairs={{0,16},{16,32},{32,48},{48,64},{64,80},{80,96},{96,112},{112,128},... | collective-permute-start | bytes 138248 | tf_op jit(solution)/shard_map/ppermute | solution.py:33
  147.4 6.2 %collective-permute-start.19 = (f32[1,90,128]{1,2,0:T(8,128)S(1)}, f32[1,90,128]{1,2,0:T(8,128)S(1)}, u32[]{:S(2)}, u32[]{:S(2)}) collective-permute-start(f32[1,90,128]{1,2,0:T(8,128)S(1)} %get-tuple-element.36), channel_id=1, source_target_pairs={{16,0},{32,16},{48,32},{64,48},{80,64},{96,80},{112,96},{128,112},... | collective-permute-start | bytes 138248 | tf_op jit(solution)/shard_map/ppermute | solution.py:33
  159.4 8.2 %collective-permute-start.20 = (f32[22,1,128]{2,1,0:T(1,128)S(1)}, f32[22,1,128]{2,1,0:T(1,128)S(1)}, u32[]{:S(2)}, u32[]{:S(2)}) collective-permute-start(f32[22,1,128]{2,1,0:T(1,128)S(1)} %copy.52), channel_id=1, source_target_pairs={{0,1},{1,2},{2,3},{3,4},{4,5},{5,6},{6,7},{7,8},{8,9},{9,10},{10,1... | collective-permute-start | bytes 33800 | tf_op jit(solution)/shard_map/ppermute | solution.py:33
  166.2 7.4 %collective-permute-start.21 = (f32[22,1,128]{2,1,0:T(1,128)S(1)}, f32[22,1,128]{2,1,0:T(1,128)S(1)}, u32[]{:S(2)}, u32[]{:S(2)}) collective-permute-start(f32[22,1,128]{2,1,0:T(1,128)S(1)} %copy.54), channel_id=1, source_target_pairs={{1,0},{2,1},{3,2},{4,3},{5,4},{6,5},{7,6},{8,7},{9,8},{10,9},{11,1... | collective-permute-start | bytes 33800 | tf_op jit(solution)/shard_map/ppermute | solution.py:33
  177.5 5.7 %collective-permute-start.22 = (f32[1,90,128]{1,2,0:T(8,128)S(1)}, f32[1,90,128]{1,2,0:T(8,128)S(1)}, u32[]{:S(2)}, u32[]{:S(2)}) collective-permute-start(f32[1,90,128]{1,2,0:T(8,128)S(1)} %get-tuple-element.31), channel_id=1, source_target_pairs={{0,16},{16,32},{32,48},{48,64},{64,80},{80,96},{96,112},{112,128},... | collective-permute-start | bytes 138248 | tf_op jit(solution)/shard_map/ppermute | solution.py:33
  181.2 6.5 %collective-permute-start.23 = (f32[1,90,128]{1,2,0:T(8,128)S(1)}, f32[1,90,128]{1,2,0:T(8,128)S(1)}, u32[]{:S(2)}, u32[]{:S(2)}) collective-permute-start(f32[1,90,128]{1,2,0:T(8,128)S(1)} %get-tuple-element.32), channel_id=1, source_target_pairs={{16,0},{32,16},{48,32},{64,48},{80,64},{96,80},{112,96},{128,112},... | collective-permute-start | bytes 138248 | tf_op jit(solution)/shard_map/ppermute | solution.py:33
  193.5 8.4 %collective-permute-start.24 = (f32[22,1,128]{2,1,0:T(1,128)S(1)}, f32[22,1,128]{2,1,0:T(1,128)S(1)}, u32[]{:S(2)}, u32[]{:S(2)}) collective-permute-start(f32[22,1,128]{2,1,0:T(1,128)S(1)} %copy.56), channel_id=1, source_target_pairs={{0,1},{1,2},{2,3},{3,4},{4,5},{5,6},{6,7},{7,8},{8,9},{9,10},{10,1... | collective-permute-start | bytes 33800 | tf_op jit(solution)/shard_map/ppermute | solution.py:33
  200.6 5.3 %collective-permute-start.25 = (f32[22,1,128]{2,1,0:T(1,128)S(1)}, f32[22,1,128]{2,1,0:T(1,128)S(1)}, u32[]{:S(2)}, u32[]{:S(2)}) collective-permute-start(f32[22,1,128]{2,1,0:T(1,128)S(1)} %copy.58), channel_id=1, source_target_pairs={{1,0},{2,1},{3,2},{4,3},{5,4},{6,5},{7,6},{8,7},{9,8},{10,9},{11,1... | collective-permute-start | bytes 33800 | tf_op jit(solution)/shard_map/ppermute | solution.py:33
  209.8 5.2 %collective-permute-start.26 = (f32[1,90,128]{1,2,0:T(8,128)S(1)}, f32[1,90,128]{1,2,0:T(8,128)S(1)}, u32[]{:S(2)}, u32[]{:S(2)}) collective-permute-start(f32[1,90,128]{1,2,0:T(8,128)S(1)} %get-tuple-element.27), channel_id=1, source_target_pairs={{0,16},{16,32},{32,48},{48,64},{64,80},{80,96},{96,112},{112,128},... | collective-permute-start | bytes 138248 | tf_op jit(solution)/shard_map/ppermute | solution.py:33
  213.1 6.5 %collective-permute-start.27 = (f32[1,90,128]{1,2,0:T(8,128)S(1)}, f32[1,90,128]{1,2,0:T(8,128)S(1)}, u32[]{:S(2)}, u32[]{:S(2)}) collective-permute-start(f32[1,90,128]{1,2,0:T(8,128)S(1)} %get-tuple-element.28), channel_id=1, source_target_pairs={{16,0},{32,16},{48,32},{64,48},{80,64},{96,80},{112,96},{128,112},... | collective-permute-start | bytes 138248 | tf_op jit(solution)/shard_map/ppermute | solution.py:33
  225.4 85.8 %collective-permute-start.28 = (f32[22,1,128]{2,1,0:T(1,128)S(1)}, f32[22,1,128]{2,1,0:T(1,128)S(1)}, u32[]{:S(2)}, u32[]{:S(2)}) collective-permute-start(f32[22,1,128]{2,1,0:T(1,128)S(1)} %copy.60), channel_id=1, source_target_pairs={{0,1},{1,2},{2,3},{3,4},{4,5},{5,6},{6,7},{7,8},{8,9},{9,10},{10,1... | collective-permute-start | bytes 33800 | tf_op jit(solution)/shard_map/ppermute | solution.py:33
  231.2 80.4 %collective-permute-start.29 = (f32[22,1,128]{2,1,0:T(1,128)S(1)}, f32[22,1,128]{2,1,0:T(1,128)S(1)}, u32[]{:S(2)}, u32[]{:S(2)}) collective-permute-start(f32[22,1,128]{2,1,0:T(1,128)S(1)} %copy.62), channel_id=1, source_target_pairs={{1,0},{2,1},{3,2},{4,3},{5,4},{6,5},{7,6},{8,7},{9,8},{10,9},{11,1... | collective-permute-start | bytes 33800 | tf_op jit(solution)/shard_map/ppermute | solution.py:33
  315.5 5.1 %collective-permute-start.30 = (f32[1,90,128]{1,2,0:T(8,128)S(1)}, f32[1,90,128]{1,2,0:T(8,128)S(1)}, u32[]{:S(2)}, u32[]{:S(2)}) collective-permute-start(f32[1,90,128]{1,2,0:T(8,128)S(1)} %get-tuple-element.23), channel_id=1, source_target_pairs={{0,16},{16,32},{32,48},{48,64},{64,80},{80,96},{96,112},{112,128},... | collective-permute-start | bytes 138248 | tf_op jit(solution)/shard_map/ppermute | solution.py:33
  318.1 5.6 %collective-permute-start.31 = (f32[1,90,128]{1,2,0:T(8,128)S(1)}, f32[1,90,128]{1,2,0:T(8,128)S(1)}, u32[]{:S(2)}, u32[]{:S(2)}) collective-permute-start(f32[1,90,128]{1,2,0:T(8,128)S(1)} %get-tuple-element.24), channel_id=1, source_target_pairs={{16,0},{32,16},{48,32},{64,48},{80,64},{96,80},{112,96},{128,112},... | collective-permute-start | bytes 138248 | tf_op jit(solution)/shard_map/ppermute | solution.py:33
  323.7 1.5 copy-start.1
where the time goes:
time: 327 us; the launch traced here: 325 us
  starting transfers between devices  102 us (31%)
  blocking collectives  78.3 us (24%)
  local copies, waits for them, and re-layouts  60.6 us (19%)
  waiting for transfers between devices  42.6 us (13%)
  other arithmetic  32.2 us (10%)
  matrix products  8.47 us (3%)
    psum x1, blocking collectives, shards(): growth_grad = lax.psum(growth_bar, ('lat', 'lon')) / cell_count  78.3 us
    ppermute x16, starting transfers between devices, from_behind(): return lax.ppermute(value, axis, pairs)  50.3 us
    ppermute x8, starting transfers between devices, with_halo(): lax.ppermute(tail, axis, [(i, (i + 1) % count) for i in range(ends)])  37.7 us
    ppermute x16, waiting for transfers between devices, from_behind(): return lax.ppermute(value, axis, pairs)  30.9 us
    slice x12, local copies, waits for them, and re-layouts, with_halo(): head = lax.slice_in_dim(cells, 0, width, axis=dim)  14.6 us
    slice x8, local copies, waits for them, and re-layouts, along_lon(): blocks[:, margin_width + core_cols:]  13.7 us
    ppermute x8, starting transfers between devices, with_halo(): lax.ppermute(head, axis, [((i + 1) % count, i) for i in range(ends)])  13.5 us
    mul x4, other arithmetic, advance(): return wet_channels * summed  11.7 us
  transfers between devices with their start and end apart: 32, of which 11 were waited for; matrix products, arithmetic and copies ran while one was open for 7% of the time, Pallas kernels for 0%

commit v1 on v0

v1 whole, which is shorter than its diff:
```python
import jax
import jax.numpy as jnp
from jax import lax
from jax.experimental import pallas as pl
from jax.experimental.pallas import tpu as pltpu
from jax.sharding import PartitionSpec as P

TRACERS = 64
PHYTO = 35
NUTRIENTS = 4
ORGANIC = 25
LEVELS = 2
SUBSTEPS = 4
ROWS_DEV = 20
COLS_DEV = 90
CHANNELS = 128
FIRST_P = NUTRIENTS
FIRST_O = NUTRIENTS + PHYTO


HALO = SUBSTEPS
ALL_ROWS = ROWS_DEV + 2 * HALO
BLOCKS = 13
COLS_PAD = 8 * BLOCKS
LEFT = 8
RIGHT = LEFT + COLS_DEV
ROW = (BLOCKS, 8, CHANNELS)
GROUP = 4
GROUPS = ROWS_DEV // GROUP
GROUP_CELLS = GROUP * COLS_PAD
KINDS = 6
CODES = NUTRIENTS + 1
CELLS = 320 * 1440 * LEVELS
MESH = pl.DeviceIdType.MESH
SENT = (3, 2, 3)
MOVES = ((-1, 0), (1, 0), (0, -1), (0, 1), (-1, -1), (-1, 1), (1, -1), (1, 1))
INNER_LOOPS = (0, 3, 2, 2, 2)
RADIX = 4
NEAR = RADIX * RADIX
F32 = jnp.float32
BF16 = jnp.bfloat16


def split(value):
    high = value.astype(BF16)
    low = (value - high.astype(F32)).astype(BF16)
    return jnp.concatenate([high, low], axis=1)


def dot(a, b):
    return jnp.dot(a, b, preferred_element_type=F32)


def cell(column):
    return column % BLOCKS, column // BLOCKS


def blocked(jj):
    return pl.ds(jj, 8, stride=BLOCKS)


def forward_block(weights, dst, src, i, count):
    above = [src[i - 1, jj] for jj in range(BLOCKS)]
    rows = [[src[i + d, jj] for jj in range(BLOCKS)] for d in range(count)]
    under = [src[i + count, jj] for jj in range(BLOCKS)]
    rows = [above] + rows + [under]
    for jj in range(BLOCKS):
        for d in range(count):
            row = rows[d + 1]
            east = row[jj + 1] if jj < BLOCKS - 1 else pltpu.roll(row[0], 7, 0)
            west = row[jj - 1] if jj > 0 else pltpu.roll(row[BLOCKS - 1], 1, 0)
            total = weights[0, i + d, jj] * row[jj]
            total += weights[1, i + d, jj] * east
            total += weights[2, i + d, jj] * west
            total += weights[3, i + d, jj] * rows[d + 2][jj]
            total += weights[4, i + d, jj] * rows[d][jj]
            dst[i + d, jj] = total


def backward_block(weights, put, src, i, count):
    rows = [[src[i + d, jj] for jj in range(BLOCKS)] for d in range(-1, count + 1)]
    for jj in range(BLOCKS):
        for d in range(count):
            row = rows[d + 1]
            if jj > 0:
                from_west = weights[1, i + d, jj - 1] * row[jj - 1]
            else:
                from_west = pltpu.roll(weights[1, i + d, BLOCKS - 1] * row[BLOCKS - 1], 1, 0)
            if jj < BLOCKS - 1:
                from_east = weights[2, i + d, jj + 1] * row[jj + 1]
            else:
                from_east = pltpu.roll(weights[2, i + d, 0] * row[0], 7, 0)
            total = weights[0, i + d, jj] * row[jj]
            total += weights[3, i + d - 1, jj] * rows[d][jj]
            total += weights[4, i + d + 1, jj] * rows[d + 2][jj]
            put(i + d, jj, total + (from_west + from_east))


def outer_rows(block, weights, to, src, step):
    block(weights, to, src, step, HALO)
    block(weights, to, src, ALL_ROWS - HALO - step, HALO)


def into(dst):
    def put(i, jj, total):
        dst[i, jj] = total

    return put


def kernel(
    state_hbm,
    cot_hbm,
    codes_hbm,
    center_hbm,
    sides_hbm,
    growth_hbm,
    mortality_hbm,
    sinking_hbm,
    remineral_hbm,
    half_sat_hbm,
    stoich_hbm,
    routing_hbm,
    release_hbm,
    result,
    totals,
    state,
    cot,
    codes,
    center,
    sides,
    growth,
    mortality,
    sinking,
    remineral,
    half_sat,
    stoich,
    routing,
    release,
    kinds,
    kinds_t,
    vectors,
    pieces,
    hot,
    halves,
    carried,
    parts,
    bar0,
    drive,
    picked,
    pull,
    weights,
    v,
    b,
    acc,
    row_out,
    row_in,
    col_out,
    col_in,
    corner_out,
    corner_in,
    gather,
    load_sem,
    send_sem,
    recv_sem,
    gsend_sem,
    grecv_sem,
):
    lat, lon = lax.axis_index("lat"), lax.axis_index("lon")
    n_lat, n_lon = lax.axis_size("lat"), lax.axis_size("lon")

    def there(move):
        i, j = lat + move[0], lon + move[1]
        return (i >= 0) & (i < n_lat) & (j >= 0) & (j < n_lon)

    def back(move):
        return there((-move[0], -move[1]))

    lat_low, lat_high = lax.rem(lat, RADIX), lax.div(lat, RADIX)
    lon_low, lon_high = lax.rem(lon, RADIX), lax.div(lon, RADIX)
    places = (lat_high * RADIX + lon_high, lat_low * RADIX + lon_low)

    def peer(stage, turn):
        index = lax.rem(places[stage] + turn, NEAR)
        high, low = lax.div(index, RADIX), lax.rem(index, RADIX)
        if stage == 0:
            return index, (high * RADIX + lat_low, low * RADIX + lon_low)
        return index, (lat_high * RADIX + high, lon_high * RADIX + low)

    inner = pl.ds(LEFT, COLS_DEV)
    sources = (
        (codes_hbm, codes),
        (center_hbm, center),
        (sides_hbm, sides),
        (state_hbm, state.at[:, inner, :]),
        (cot_hbm, cot.at[:, inner, :]),
        (growth_hbm, growth),
        (mortality_hbm, mortality),
        (sinking_hbm, sinking),
        (remineral_hbm, remineral),
        (half_sat_hbm, half_sat),
        (stoich_hbm, stoich),
        (routing_hbm, routing),
        (release_hbm, release),
    )
    loads = [
        pltpu.make_async_copy(source, target, load_sem.at[n])
        for n, (source, target) in enumerate(sources)
    ]
    for load in loads:
        load.start()

    barrier = pltpu.get_barrier_semaphore()
    count = jnp.int32(2 * (NEAR - 1))
    for move in MOVES:
        near = there(move)
        count = count + near.astype(jnp.int32)

        @pl.when(near)
        def _():
            pl.semaphore_signal(
                barrier, inc=1, device_id=(lat + move[0], lon + move[1]), device_id_type=MESH
            )

    for stage in range(2):

        @pl.loop(1, NEAR)
        def _(turn):
            pl.semaphore_signal(
                barrier, inc=1, device_id=peer(stage, turn)[1], device_id_type=MESH
            )

    for which, move in enumerate(MOVES):

        @pl.when(jnp.logical_not(back(move)))
        def _():
            for phase in range(3):
                if which < 2:
                    for r in range(SENT[phase]):
                        row_in[phase, which, r, LEFT:RIGHT] = jnp.zeros((COLS_DEV, CHANNELS), F32)
                elif which < 4:
                    col_in[phase, which - 2] = jnp.zeros_like(col_in[phase, which - 2])
                elif phase != 1:
                    corner_in[phase, which - 4] = jnp.zeros_like(corner_in[phase, which - 4])

    left_zeros = jnp.zeros((LEFT, CHANNELS), F32)
    right_zeros = jnp.zeros((COLS_PAD - RIGHT, CHANNELS), F32)

    @pl.loop(0, ROWS_DEV)
    def _(i):
        state[i, 0:LEFT] = left_zeros
        state[i, RIGHT:COLS_PAD] = right_zeros
        cot[i, 0:LEFT] = left_zeros
        cot[i, RIGHT:COLS_PAD] = right_zeros

    for phase in range(3):
        for which in range(2):
            for r in range(SENT[phase]):
                row_in[phase, which, r, 0:LEFT] = left_zeros
                row_in[phase, which, r, RIGHT:COLS_PAD] = right_zeros
    corner_out[...] = jnp.zeros_like(corner_out)

    kinds[...] = jnp.zeros_like(kinds)
    kinds_t[...] = jnp.zeros_like(kinds_t)
    for load in loads[:3]:
        load.wait()
    upper_code, lower_code = codes[:, 0, :], codes[:, 1, :]
    wet = (upper_code != NUTRIENTS).astype(F32)
    every = lambda k: pl.ds(k, ROWS_DEV, stride=KINDS)
    kinds[every(0), 0:COLS_DEV] = wet * center[...]
    for s in range(4):
        kinds[every(s + 1), 0:COLS_DEV] = wet * sides[:, s, :]
    kinds[every(5), 0:COLS_DEV] = (upper_code + CODES * lower_code).astype(F32)
    kinds_t[LEFT:RIGHT] = kinds[...].T[0:COLS_DEV]

    lane = lax.broadcasted_iota(jnp.int32, (1, CHANNELS), 1)
    lane_in = lax.rem(lane, TRACERS)
    organic = lane_in >= FIRST_O
    loads[3].wait()

    def carry(i, low, high):
        turned = pltpu.roll(kinds_t[low:high], (FIRST_O - KINDS * i) % CHANNELS, 1)
        wide = jnp.broadcast_to(turned[:, FIRST_O : FIRST_O + 1], (high - low, CHANNELS))
        masked = jnp.where(wide > 0, state[i, low:high], 0.0)
        state[i, low:high] = jnp.where(organic, turned, masked)

    for i in range(ROWS_DEV):
        if i < HALO or i >= ROWS_DEV - HALO:
            carry(i, 0, COLS_PAD)
        else:
            carry(i, LEFT, LEFT + 8)
            carry(i, 88, COLS_PAD)

    lane_free = lane_in >= FIRST_O + 5

    def turn_by(value, shift):
        return pltpu.roll(value, shift % CHANNELS, 1)

    def pack_state(cells):
        return [
            jnp.where(lane_free, turn_by(cells[3], FIRST_O + 5 - 20 * n), cells[n]) for n in range(3)
        ]

    def unpack_state(sent_cells):
        last = [turn_by(sent_cells[n], 20 * n - FIRST_O - 5) for n in range(3)]
        last = jnp.where(lane_in < 20, last[0], jnp.where(lane_in < 40, last[1], last[2]))
        return list(sent_cells) + [last]

    def pack_organic(cells):
        return [jnp.where(organic, cells[n], turn_by(cells[n + 2], -FIRST_O)) for n in range(2)]

    def pack_bars(cells):
        return [
            jnp.where(organic, turn_by(cells[3], FIRST_O), cells[0]),
            jnp.where(organic, turn_by(cells[3], FIRST_O - ORGANIC), cells[1]),
            cells[2],
        ]

    def unpack_bars(sent_cells, sent_organic):
        last = jnp.where(
            lane_in < ORGANIC,
            turn_by(sent_cells[0], -FIRST_O),
            turn_by(sent_cells[1], ORGANIC - FIRST_O),
        )
        others = list(sent_organic) + [turn_by(cells, FIRST_O) for cells in sent_organic]
        return [
            jnp.where(organic, other, cells)
            for other, cells in zip(others, list(sent_cells) + [last])
        ]

    def received_cols(phase, side):
        cells = [col_in[phase, side, n] for n in range(3)]
        if phase == 0:
            return unpack_state(cells)
        return unpack_bars(cells, [col_in[1, side, n] for n in range(2)])

    def received_rows(phase, which, jj):
        cells = [row_in[phase, which, n, blocked(jj), :] for n in range(3)]
        if phase == 0:
            return unpack_state(cells)
        return unpack_bars(cells, [row_in[1, which, n, blocked(jj), :] for n in range(2)])

    def message(phase, which):
        move = MOVES[which]
        sent_rows = pl.ds(0, SENT[phase])
        if which < 2:
            source = row_out.at[phase, which, sent_rows, inner, :]
            target = row_in.at[phase, which, sent_rows, inner, :]
        elif which < 4:
            source = col_out.at[phase, which - 2, sent_rows]
            target = col_in.at[phase, which - 2, sent_rows]
        else:
            source, target = corner_out.at[phase, which - 4], corner_in.at[phase, which - 4]
        return pltpu.make_async_remote_copy(
            src_ref=source,
            dst_ref=target,
            send_sem=send_sem.at[phase, which],
            recv_sem=recv_sem.at[phase, which],
            device_id=(lat + move[0], lon + move[1]),
            device_id_type=MESH,
        )

    def send(phase, which):
        @pl.when(there(MOVES[which]))
        def _():
            message(phase, which).start()

    def sent(phase, which):
        @pl.when(there(MOVES[which]))
        def _():
            message(phase, which).wait_send()

    def arrived(phase, which):
        @pl.when(back(MOVES[which]))
        def _():
            message(phase, which).wait_recv()

    def corner_cells(which, inside):
        down, right = MOVES[4 + which]
        at = 0
        for depth in range(3):
            for t in range(3 - depth):
                if inside:
                    row = depth if down < 0 else ROWS_DEV - 1 - depth
                    column = LEFT + t if right < 0 else RIGHT - 1 - t
                else:
                    row = ROWS_DEV + depth if down < 0 else -1 - depth
                    column = RIGHT + t if right < 0 else LEFT - 1 - t
                yield at, row, column
                at += 1

    weight_cells = weights.reshape(5 * ALL_ROWS * COLS_PAD, CHANNELS)

    def column_cells(jj, s, base=0):
        return pl.ds(base + HALO * COLS_PAD + 8 * jj + s, ROWS_DEV, stride=COLS_PAD)

    def unpack_cols(phase, field):
        cells = field.reshape(ALL_ROWS * COLS_PAD, CHANNELS)
        for side in range(2):
            halo = received_cols(phase, side)
            for t in range(HALO):
                jj, s = cell(RIGHT + t if side == 0 else LEFT - HALO + t)
                cells[column_cells(jj, s), :] = halo[t]
                for k in range(5 if phase == 0 else 0):
                    weight_cells[column_cells(jj, s, k * ALL_ROWS * COLS_PAD), :] = (
                        jnp.broadcast_to(
                            halo[t][:, FIRST_O + k : FIRST_O + k + 1], (ROWS_DEV, CHANNELS)
                        )
                    )

    def unpack_rows(phase, field):
        for which in range(2):
            first = ALL_ROWS - HALO if which == 0 else 0
            for jj in range(BLOCKS):
                for r, cells in enumerate(received_rows(phase, which, jj)):
                    field[first + r, jj] = cells

        for which in range(4):
            for at, row, column in corner_cells(which, False):
                jj, s = cell(column)
                field[HALO + row, jj, s : s + 1, :] = corner_in[phase, which, at : at + 1, :]

    state_cells = state.reshape(ROWS_DEV * COLS_PAD, CHANNELS)
    for side in range(2):
        at = LEFT if side == 0 else RIGHT - HALO
        cells = [state_cells[pl.ds(at + t, ROWS_DEV, stride=COLS_PAD), :] for t in range(HALO)]
        for n, value in enumerate(pack_state(cells)):
            col_out[0, side, n] = value
    for which in range(2):
        first = 0 if which == 0 else ROWS_DEV - HALO
        for n, value in enumerate(pack_state([state[first + r] for r in range(HALO)])):
            row_out[0, which, n] = value

    for which in range(4):
        for at, row, column in corner_cells(which, True):
            corner_out[0, which, at : at + 1] = state[row, column : column + 1]

    order = (2, 3, 0, 1, 4, 5, 6, 7)
    pl.semaphore_wait(barrier, count)
    for which in order:
        send(0, which)

    v0 = v.at[0]

    lane_f = lane_in.astype(F32)
    upper = lane < TRACERS

    for load in loads[5:]:
        load.wait()
    vectors[...] = jnp.zeros_like(vectors)
    pieces[...] = jnp.zeros_like(pieces)
    for l in range(LEVELS):
        n, p, o = l * TRACERS, l * TRACERS + FIRST_P, l * TRACERS + FIRST_O
        end = (l + 1) * TRACERS
        vectors[0:1, p:o] = growth[...]
        vectors[1:2, p:o] = mortality[...]
        vectors[2:3, p:o] = sinking[...]
        vectors[3:4, o:end] = remineral[...]
        pieces[0, n : n + NUTRIENTS, p:o] = stoich[...]
        pieces[1, o:end, p:o] = routing[...]
        pieces[2, n : n + NUTRIENTS, o:end] = release[...]
        pieces[3, n : n + NUTRIENTS, p:o] = half_sat[...]
    rate, lost, sunk, decayed = (vectors[n : n + 1, :] for n in range(4))

    row_lane = lax.broadcasted_iota(jnp.int32, (CHANNELS, CHANNELS), 0)
    col_lane = lax.broadcasted_iota(jnp.int32, (CHANNELS, CHANNELS), 1)
    same = (row_lane < TRACERS) == (col_lane < TRACERS)
    row_in_level = lax.rem(row_lane, TRACERS)
    col_in_level = lax.rem(col_lane, TRACERS)
    row_p = (row_in_level >= FIRST_P) & (row_in_level < FIRST_O)
    col_p = (col_in_level >= FIRST_P) & (col_in_level < FIRST_O)
    own = jnp.where(row_lane == col_lane, 1.0, 0.0)
    own_p = jnp.where((row_lane == col_lane) & col_p, 1.0, 0.0)
    below = jnp.where(row_lane == col_lane + TRACERS, 1.0, 0.0)
    bars = own * ((1.0 - lost) * (1.0 - sunk) * (1.0 - decayed))
    bars += below * ((1.0 - lost) * sunk) + pieces[1] * lost + pieces[2] * decayed
    light = jnp.where(upper, 1.0, 0.4)
    drives = light * (own_p * (1.0 - sunk) + below * sunk - pieces[0])
    ones = jnp.where(col_p[0:1], 0.0, 1.0)
    halves_of = [pieces[3, k : k + 1, :] + pieces[3, TRACERS + k : TRACERS + k + 1, :] + ones for k in range(NUTRIENTS)]
    pick = jnp.where(same & (row_in_level < NUTRIENTS) & col_p, 1.0, 0.0).astype(BF16)
    collect = jnp.where(same & (col_in_level < NUTRIENTS) & row_p, 1.0, 0.0).astype(BF16)
    pick = jnp.concatenate([pick, pick], axis=0)
    collect = jnp.concatenate([collect, collect], axis=0)
    maps = jnp.concatenate([bars, drives], axis=1)
    maps_high = maps.astype(BF16)
    maps_low = (maps - maps_high.astype(F32)).astype(BF16)
    maps_twice = jnp.concatenate([maps_high, maps_high], axis=0)

    for i in range(HALO, ROWS_DEV - HALO):
        turned = pltpu.roll(kinds_t[16:88], (FIRST_O - KINDS * i) % CHANNELS, 1)
        state[i, 16:88] = jnp.where(organic, turned, state[i, 16:88])
    spread = jnp.concatenate(
        [jnp.where(row_lane == FIRST_O + k, 1.0, 0.0).astype(BF16) for k in range(5)], axis=1
    )
    spread = jnp.concatenate([spread, spread], axis=0)
    for n in range(ROWS_DEV // 2):
        block = jnp.concatenate(
            [state[2 * n + r, blocked(jj), :] for r in range(2) for jj in range(BLOCKS)], axis=0
        )
        carried[2 * COLS_PAD * n : 2 * COLS_PAD * (n + 1)] = split(block)
    for g in range(GROUPS):
        cells = pl.ds(GROUP_CELLS * g, GROUP_CELLS)
        wide = dot(carried[cells], spread)
        for k in range(5):
            part = wide[:, CHANNELS * k : CHANNELS * (k + 1)]
            weights[k, HALO + GROUP * g : HALO + GROUP * (g + 1)] = part.reshape((GROUP,) + ROW)
        for i in range(GROUP * g, GROUP * (g + 1)):
            for jj in range(BLOCKS):
                cells = state[i, blocked(jj), :]
                v0[HALO + i, jj] = jnp.where(weights[0, HALO + i, jj] > 0, cells, 0.0)
                code = jnp.broadcast_to(cells[:, FIRST_O + 5 : FIRST_O + 6], (8, CHANNELS))
                second = jnp.floor((code + 0.5) * (1.0 / CODES))
                here = jnp.where(upper, code - CODES * second, second)
                hot[i, jj] = jnp.where(here == lane_f, 1.0, 0.0)
                halved = jnp.ones((8, CHANNELS), F32)
                for k in range(NUTRIENTS):
                    halved = jnp.where(here == k, halves_of[k], halved)
                halves[i, jj] = halved

    loads[4].wait()
    for n in range(ROWS_DEV // 2):
        block = jnp.concatenate(
            [cot[2 * n + r, blocked(jj), :] for r in range(2) for jj in range(BLOCKS)], axis=0
        )
        parts[2 * COLS_PAD * n : 2 * COLS_PAD * (n + 1)] = split(block)
    for n in range(GROUPS):
        cells = pl.ds(GROUP_CELLS * n, GROUP_CELLS)
        both = dot(parts[cells], maps_twice) + dot(parts[cells, 0:CHANNELS], maps_low)
        bar0[cells] = both[:, :CHANNELS]
        drive[cells] = both[:, CHANNELS:]

    for side in range(2):
        cells = []
        for t in range(HALO):
            jj, s = cell(LEFT + t if side == 0 else RIGHT - HALO + t)
            cells.append(bar0[pl.ds(8 * jj + s, ROWS_DEV, stride=COLS_PAD), :])
        for n, value in enumerate(pack_organic(cells)):
            col_out[1, side, n] = value
    for which in range(2):
        first = 0 if which == 0 else ROWS_DEV - HALO
        for jj in range(BLOCKS):
            cells = [
                bar0[COLS_PAD * (first + r) + 8 * jj : COLS_PAD * (first + r) + 8 * jj + 8]
                for r in range(HALO)
            ]
            for n, value in enumerate(pack_organic(cells)):
                row_out[1, which, n, blocked(jj), :] = value
    for which in range(4):
        send(1, which)

    def inner_rows(block, to, src, step):
        count = (ROWS_DEV - 2 * step) // INNER_LOOPS[step]

        @pl.loop(0, INNER_LOOPS[step])
        def _(n):
            block(weights, to, src, HALO + step + count * n, count)

    one = (COLS_PAD, CHANNELS)

    def pick_rows(rows):
        moved = [v[SUBSTEPS, HALO + r].reshape(one) * hot[r].reshape(one) for r in rows]
        chosen = dot(split(jnp.concatenate(moved, axis=0)), pick)
        for n, r in enumerate(rows):
            picked[COLS_PAD * r : COLS_PAD * (r + 1)] = chosen[COLS_PAD * n : COLS_PAD * (n + 1)]

    def uptake_row(r):
        cells = slice(COLS_PAD * r, COLS_PAD * (r + 1))
        p = v[SUBSTEPS, HALO + r].reshape(one)
        halved = halves[r].reshape(one)
        force = drive[cells]
        chosen = picked[cells]
        total = chosen + halved
        inverse = pl.reciprocal(total, approx=True)
        inverse = inverse * (2.0 - total * inverse)
        return cells, p, halved, force, inverse, force * (chosen * inverse)

    def growth_rows(rows, add, spread):
        for n, r in enumerate(rows):
            near = slice(COLS_PAD * n, COLS_PAD * (n + 1))
            cells, p, halved, force, inverse, taken = uptake_row(r)
            if add:
                acc[...] += jnp.sum((taken * p).reshape(ROW), axis=0)
            if spread:
                pull[near] = (rate * force) * p * halved * (inverse * inverse)
                b[0, HALO + r] = (bar0[cells] + rate * taken).reshape(ROW)
        if spread:
            pulled = dot(split(pull[0 : COLS_PAD * len(rows)]), collect)
            for n, r in enumerate(rows):
                part = pulled[COLS_PAD * n : COLS_PAD * (n + 1)]
                b[0, HALO + r] += part.reshape(ROW) * hot[r]

    inner_groups = [range(GROUP * g, GROUP * (g + 1)) for g in range(1, GROUPS - 1)]
    outer = list(range(HALO)) + list(range(ROWS_DEV - HALO, ROWS_DEV))

    for which in (2, 3):
        arrived(0, which)
    unpack_cols(0, v0)
    for step in range(1, SUBSTEPS + 1):
        inner_rows(forward_block, v.at[step], v.at[step - 1], step)
    acc[...] = jnp.zeros_like(acc)

    for rows in inner_groups:
        pick_rows(rows)
        growth_rows(rows, True, False)

    for which in (0, 1, 4, 5, 6, 7):
        arrived(0, which)
    unpack_rows(0, v0)

    halo_rows = list(range(HALO)) + list(range(ALL_ROWS - HALO, ALL_ROWS))
    wide = dot(split(jnp.concatenate([v0[i].reshape(one) for i in halo_rows], axis=0)), spread)
    for n, i in enumerate(halo_rows):
        for k in range(5):
            part = wide[COLS_PAD * n : COLS_PAD * (n + 1), CHANNELS * k : CHANNELS * (k + 1)]
            weights[k, i] = part.reshape(ROW)

    for step in range(1, SUBSTEPS + 1):
        outer_rows(forward_block, weights, v.at[step], v.at[step - 1], step)

    pick_rows(outer)
    growth_rows(outer, True, True)

    def exchange(stage, turn, slot):
        return pltpu.make_async_remote_copy(
            src_ref=gather.at[stage, slot],
            dst_ref=gather.at[stage, slot],
            send_sem=gsend_sem.at[stage, turn],
            recv_sem=grecv_sem.at[stage, slot],
            device_id=peer(stage, turn)[1],
            device_id_type=MESH,
        )

    def stage_start(stage, value):
        gather[stage, places[stage]] = value

        @pl.loop(1, NEAR)
        def _(turn):
            exchange(stage, turn, places[stage]).start()

    def stage_end(stage):
        @pl.loop(1, NEAR)
        def _(turn):
            exchange(stage, turn, peer(stage, turn)[0]).wait_recv()
            exchange(stage, turn, places[stage]).wait_send()

        parts = [gather[stage, n] for n in range(NEAR)]
        while len(parts) > 1:
            parts = [a + c for a, c in zip(parts[0::2], parts[1::2])]
        return parts[0]

    b0 = b.at[0]
    for which in range(4):
        for at, row, column in corner_cells(which, True):
            jj, s = cell(column)
            corner_out[2, which, at : at + 1, :] = b0[HALO + row, jj, s : s + 1, :]
    for which in range(2):
        first = HALO if which == 0 else ROWS_DEV
        for jj in range(BLOCKS):
            cells = [b0[first + r, jj] for r in range(HALO)]
            for n, value in enumerate(pack_bars(cells)):
                row_out[2, which, n, blocked(jj), :] = value
    for which in (0, 1, 4, 5, 6, 7):
        send(2, which)
    stage_start(0, jnp.sum(acc[...], axis=0, keepdims=True))

    for rows in inner_groups:
        growth_rows(rows, False, True)
    b0_cells = b0.reshape(ALL_ROWS * COLS_PAD, CHANNELS)
    for side in range(2):
        cells = []
        for t in range(HALO):
            jj, s = cell(LEFT + t if side == 0 else RIGHT - HALO + t)
            cells.append(b0_cells[column_cells(jj, s), :])
        for n, value in enumerate(pack_bars(cells)):
            col_out[2, side, n] = value
    for which in (2, 3):
        send(2, which)

    def finish(i, jj, total):
        result[i - HALO, blocked(jj), :] = jnp.where(weights[0, i, jj] > 0, total, 0.0)

    goals = [into(b.at[step]) for step in range(1, SUBSTEPS)] + [finish]
    stage_start(1, stage_end(0))
    for which in (2, 3):
        arrived(1, which)
        arrived(2, which)
    unpack_cols(2, b0)
    for step in range(1, SUBSTEPS + 1):
        inner_rows(backward_block, goals[step - 1], b.at[step - 1], step)
    for which in (0, 1):
        arrived(1, which)
    for which in (0, 1, 4, 5, 6, 7):
        arrived(2, which)
    unpack_rows(2, b0)
    for step in range(1, SUBSTEPS + 1):
        outer_rows(backward_block, weights, goals[step - 1], b.at[step - 1], step)
    for phase in range(3):
        for which in range(4 if phase == 1 else 8):
            sent(phase, which)
    totals[...] = stage_end(1)


def finish_kernel(result, totals, out, growth_out, growth, sem):
    count = ROWS_DEV // GROUPS
    copies = [
        pltpu.make_async_copy(
            result.at[pl.ds(count * n, count), pl.ds(LEFT, COLS_DEV), :],
            out.at[pl.ds(count * n, count)],
            sem.at[n],
        )
        for n in range(GROUPS)
    ]
    for copy in copies:
        copy.start()
    lanes = totals[...]
    lanes = (lanes + pltpu.roll(lanes, TRACERS, 1)) * (1.0 / CELLS)
    growth[...] = pltpu.roll(lanes, CHANNELS - FIRST_P, 1)[:, 0:PHYTO]
    copies.append(pltpu.make_async_copy(growth, growth_out, sem.at[GROUPS]))
    copies[GROUPS].start()
    for copy in copies:
        copy.wait()


def shards(
    tracer_state,
    limit_codes,
    center_weight,
    side_weights,
    growth,
    half_sat,
    stoich,
    mortality,
    sinking,
    routing,
    remineral,
    release,
    cotangent,
):
    hbm = pl.BlockSpec(memory_space=pltpu.HBM)
    vmem = pl.BlockSpec(memory_space=pltpu.VMEM)
    padded = (ROWS_DEV, COLS_PAD, CHANNELS)
    cells = (ROWS_DEV,) + ROW
    field = (ALL_ROWS,) + ROW
    halo_rows = (3, 2, 3, COLS_PAD, CHANNELS)
    operands = (
        tracer_state,
        cotangent,
        jnp.transpose(limit_codes, (1, 0, 2)),
        center_weight,
        jnp.transpose(side_weights, (1, 0, 2)),
        growth[None, :],
        mortality[None, :],
        sinking[None, :],
        remineral[None, :],
        half_sat,
        stoich,
        routing,
        release,
    )
    results = pl.pallas_call(
        kernel,
        out_shape=(
            pltpu.VMEM(padded, F32),
            pltpu.VMEM((1, CHANNELS), F32),
        ),
        in_specs=[hbm] * len(operands),
        out_specs=(vmem,) * 2,
        scratch_shapes=[
            pltpu.VMEM(padded, F32),
            pltpu.VMEM(padded, F32),
        ]
        + [pltpu.VMEM(operand.shape, operand.dtype) for operand in operands[2:]]
        + [
            pltpu.VMEM((CHANNELS, CHANNELS), F32),
            pltpu.VMEM((COLS_PAD, CHANNELS), F32),
            pltpu.VMEM((8, CHANNELS), F32),
            pltpu.VMEM((4, CHANNELS, CHANNELS), F32),
            pltpu.VMEM(cells, F32),
            pltpu.VMEM(cells, F32),
            pltpu.VMEM((ROWS_DEV * COLS_PAD, 2 * CHANNELS), BF16),
            pltpu.VMEM((ROWS_DEV * COLS_PAD, 2 * CHANNELS), BF16),
            pltpu.VMEM((ROWS_DEV * COLS_PAD, CHANNELS), F32),
            pltpu.VMEM((ROWS_DEV * COLS_PAD, CHANNELS), F32),
            pltpu.VMEM((ROWS_DEV * COLS_PAD, CHANNELS), F32),
            pltpu.VMEM((ROWS_DEV * COLS_PAD, CHANNELS), F32),
            pltpu.VMEM((5,) + field, F32),
            pltpu.VMEM((SUBSTEPS + 1,) + field, F32),
            pltpu.VMEM((SUBSTEPS,) + field, F32),
            pltpu.VMEM((8, CHANNELS), F32),
            pltpu.VMEM(halo_rows, F32),
            pltpu.VMEM(halo_rows, F32),
            pltpu.VMEM((3, 2, 3, ROWS_DEV, CHANNELS), F32),
            pltpu.VMEM((3, 2, 3, ROWS_DEV, CHANNELS), F32),
            pltpu.VMEM((3, 4, 8, CHANNELS), F32),
            pltpu.VMEM((3, 4, 8, CHANNELS), F32),
            pltpu.VMEM((2, NEAR, 1, CHANNELS), F32),
            pltpu.SemaphoreType.DMA((len(operands),)),
            pltpu.SemaphoreType.DMA((3, 8)),
            pltpu.SemaphoreType.DMA((3, 8)),
            pltpu.SemaphoreType.DMA((2, NEAR)),
            pltpu.SemaphoreType.DMA((2, NEAR)),
        ],
        compiler_params=pltpu.CompilerParams(
            collective_id=0, has_side_effects=True, vmem_limit_bytes=65500000
        ),
        cost_estimate=pl.CostEstimate(flops=10**9, bytes_accessed=3 * 10**6, transcendentals=0),
    )(*operands)
    state_grad, growth_grad = pl.pallas_call(
        finish_kernel,
        out_shape=(
            jax.ShapeDtypeStruct((ROWS_DEV, COLS_DEV, CHANNELS), F32),
            jax.ShapeDtypeStruct((1, PHYTO), F32),
        ),
        in_specs=[vmem] * 2,
        out_specs=(hbm, hbm),
        scratch_shapes=[
            pltpu.VMEM((1, PHYTO), F32),
            pltpu.SemaphoreType.DMA((GROUPS + 1,)),
        ],
        compiler_params=pltpu.CompilerParams(vmem_limit_bytes=32 * 1024 * 1024),
        cost_estimate=pl.CostEstimate(flops=10**8, bytes_accessed=10**6, transcendentals=0),
    )(*results)
    return (state_grad, growth_grad[0])


def solution(mesh):
    in_specs = (
        P("lat", "lon", None),
        P(None, "lat", "lon"),
        P("lat", "lon"),
        P(None, "lat", "lon"),
        P(),
        P(),
        P(),
        P(),
        P(),
        P(),
        P(),
        P(),
        P("lat", "lon", None),
    )
    out_specs = (P("lat", "lon", None), P())
    return jax.shard_map(shards, mesh=mesh, in_specs=in_specs, out_specs=out_specs, check_vma=False)
```

time: 327 us -> 33 us (0.10)
  starting transfers between devices: 102 us -> 0 us
  blocking collectives: 78.3 us -> 0 us
  local copies, waits for them, and re-layouts: 60.6 us -> 0 us
  waiting for transfers between devices: 42.6 us -> 0 us
  Pallas kernels: 0 us -> 32.2 us
  other arithmetic: 32.2 us -> 0 us
  matrix products: 8.47 us -> 0 us
    ppermute x32 -> x0, starting transfers between devices: 102 us -> none  [the longest x16 50.3 us: from_behind(): return lax.ppermute(value, axis, pairs)]
    psum x1 -> x0, blocking collectives: 78.3 us -> none  [shards(): growth_grad = lax.psum(growth_bar, ('lat', 'lon')) / cell_count]
    ppermute x32 -> x0, waiting for transfers between devices: 42.6 us -> none  [the longest x16 30.9 us: from_behind(): return lax.ppermute(value, axis, pairs)]
    slice x33 -> x0, local copies, waits for them, and re-layouts: 34.6 us -> none  [the longest x12 14.6 us: with_halo(): head = lax.slice_in_dim(cells, 0, width, axis=dim)]
    pallas_call x0 -> x2, Pallas kernels: none -> 32.2 us  [the longest x1 31.3 us: shards(): pl.pallas_call(kernel, out_shape=(pltpu.VMEM(padded, F32), pltpu.VMEM((1,...]
    ppermute x16 -> x0, local copies, waits for them, and re-layouts: 21.2 us -> none  [the longest x8 8.34 us: from_behind(): return lax.ppermute(value, axis, pairs)]
    mul x14 -> x0, other arithmetic: 15.6 us -> none  [the longest x4 11.7 us: advance(): return wet_channels * summed]
    add x8 -> x0, other arithmetic: 14.3 us -> none  [the longest x4 8.67 us: along_lon(): kept + jnp.pad(incoming, ((0, 0), (core_cols - margin_width, 0), (0, 0)))]
  transfers between devices with their start and end apart: 32 -> 0, of which waited for: 11 -> 0; matrix products, arithmetic and copies ran while one was open for 7% -> 0% of each run, Pallas kernels for 0% -> 0%
where the time goes in v1:
time: 33 us; the launch traced here: 32.9 us
  Pallas kernels  32.2 us (98%)
  between operations  0.64 us (2%)
    pallas_call x1, Pallas kernels, shards(): pl.pallas_call(kernel, out_shape=(pltpu.VMEM(padded, F32), pltpu.VMEM((1,...  31.3 us
    pallas_call x1, Pallas kernels, shards(): pl.pallas_call(finish_kernel, out_shape=(jax.ShapeDtypeStruct((ROWS_DEV,...  0.97 us

profile of v1, /device:TPU:1, one launch (start us, length us, event | category | flops | bytes accessed | tf_op | source)
XLA Modules:
  0.0 32.9 jit_solution(7247692435322456630)
XLA Ops:
  0.6 31.3 %shard_map.140 = (f32[20,104,128]{2,1,0:T(8,128)S(1)}, f32[1,128]{1,0:T(1,128)S(1)}) custom-call(f32[20,90,128]{2,1,0:T(8,128)} %state_hbm.1, f32[20,90,128]{2,1,0:T(8,128)} %cot_hbm.1, s32[20,2,90]{2,1,0:T(2,128)} %bitcast.8, f32[20,90]{1,0:T(8,128)} %center_hbm.1, f32[20,4,90]{2,1,0:T(4,128)} %bitcast.7, f32[1,35]{1,0:T(1,128)} %bitcast.9, ...), custom_call_target="tpu_custom_call" | custom-call | flops 1000000000 | bytes 3000000 | tf_op jit(solution)/shard_map/pallas_call | solution.py:761
  31.9 1.0 %shard_map.141 = (f32[20,90,128]{2,1,0:T(8,128)}, f32[1,35]{1,0:T(1,128)}) custom-call(f32[20,104,128]{2,1,0:T(8,128)S(1)} %get-tuple-element.6.result, f32[1,128]{1,0:T(1,128)S(1)} %get-tuple-element.7.totals), custom_call_target="tpu_custom_call" | custom-call | flops 100000000 | bytes 1000000 | tf_op jit(solution)/shard_map/pallas_call | solution.py:809

commit v2 on v1

--- a/solution.py
+++ b/solution.py
@@ -32,7 +32,7 @@
 CODES = NUTRIENTS + 1
 CELLS = 320 * 1440 * LEVELS
 MESH = pl.DeviceIdType.MESH
-SENT = (3, 2, 3)
+SENT = (3, 1, 3)
 MOVES = ((-1, 0), (1, 0), (0, -1), (0, 1), (-1, -1), (-1, 1), (1, -1), (1, 1))
 INNER_LOOPS = (0, 3, 2, 2, 2)
 RADIX = 4
@@ -306,39 +306,49 @@
         last = jnp.where(lane_in < 20, last[0], jnp.where(lane_in < 40, last[1], last[2]))
         return list(sent_cells) + [last]
 
+    first_part = FIRST_O + TRACERS - 2 * ORGANIC
+
     def pack_organic(cells):
-        return [jnp.where(organic, cells[n], turn_by(cells[n + 2], -FIRST_O)) for n in range(2)]
+        others = jnp.where(
+            lane_in >= first_part - FIRST_O,
+            turn_by(cells[1], -ORGANIC),
+            turn_by(cells[2], -FIRST_O),
+        )
+        return [jnp.where(organic, cells[0], others)]
 
     def pack_bars(cells):
+        second = jnp.where(organic, turn_by(cells[3], FIRST_O - ORGANIC), cells[1])
         return [
             jnp.where(organic, turn_by(cells[3], FIRST_O), cells[0]),
-            jnp.where(organic, turn_by(cells[3], FIRST_O - ORGANIC), cells[1]),
-            cells[2],
+            jnp.where(lane_in >= first_part, cells[2], second),
+            jnp.where(organic, cells[3], cells[2]),
         ]
 
-    def unpack_bars(sent_cells, sent_organic):
+    def unpack_bars(sent_cells, early):
+        third = jnp.where(organic, turn_by(early, FIRST_O), sent_cells[2])
         last = jnp.where(
             lane_in < ORGANIC,
             turn_by(sent_cells[0], -FIRST_O),
             turn_by(sent_cells[1], ORGANIC - FIRST_O),
         )
-        others = list(sent_organic) + [turn_by(cells, FIRST_O) for cells in sent_organic]
         return [
-            jnp.where(organic, other, cells)
-            for other, cells in zip(others, list(sent_cells) + [last])
+            jnp.where(organic, early, sent_cells[0]),
+            jnp.where(organic, turn_by(early, ORGANIC), sent_cells[1]),
+            jnp.where(lane_in >= first_part, sent_cells[1], third),
+            jnp.where(organic, sent_cells[2], last),
         ]
 
     def received_cols(phase, side):
         cells = [col_in[phase, side, n] for n in range(3)]
         if phase == 0:
             return unpack_state(cells)
-        return unpack_bars(cells, [col_in[1, side, n] for n in range(2)])
+        return unpack_bars(cells, col_in[1, side, 0])
 
     def received_rows(phase, which, jj):
         cells = [row_in[phase, which, n, blocked(jj), :] for n in range(3)]
         if phase == 0:
             return unpack_state(cells)
-        return unpack_bars(cells, [row_in[1, which, n, blocked(jj), :] for n in range(2)])
+        return unpack_bars(cells, row_in[1, which, 0, blocked(jj), :])
 
     def message(phase, which):
         move = MOVES[which]
@@ -649,6 +659,7 @@
             parts = [a + c for a, c in zip(parts[0::2], parts[1::2])]
         return parts[0]
 
+    stage_start(0, jnp.sum(acc[...], axis=0, keepdims=True))
     b0 = b.at[0]
     for which in range(4):
         for at, row, column in corner_cells(which, True):
@@ -662,7 +673,6 @@
                 row_out[2, which, n, blocked(jj), :] = value
     for which in (0, 1, 4, 5, 6, 7):
         send(2, which)
-    stage_start(0, jnp.sum(acc[...], axis=0, keepdims=True))
 
     for rows in inner_groups:
         growth_rows(rows, False, True)

time: 33 us -> 32.6 us (0.988)
  Pallas kernels: 32.2 us -> 31.8 us
    pallas_call x1, Pallas kernels: 31.3 us -> 30.9 us  [shards(): pl.pallas_call(kernel, out_shape=(pltpu.VMEM(padded, F32), pltpu.VMEM((1,...]
where the time goes in v2:
time: 32.6 us; the launch traced here: 32.5 us
  Pallas kernels  31.8 us (98%)
  between operations  0.64 us (2%)
    pallas_call x1, Pallas kernels, shards(): pl.pallas_call(kernel, out_shape=(pltpu.VMEM(padded, F32), pltpu.VMEM((1,...  30.9 us
    pallas_call x1, Pallas kernels, shards(): pl.pallas_call(finish_kernel, out_shape=(jax.ShapeDtypeStruct((ROWS_DEV,...  0.97 us

profile of v2, /device:TPU:1, one launch (start us, length us, event | category | flops | bytes accessed | tf_op | source)
XLA Modules:
  0.0 32.5 jit_solution(12874993017012457870)
XLA Ops:
  0.6 30.9 %shard_map.140 = (f32[20,104,128]{2,1,0:T(8,128)S(1)}, f32[1,128]{1,0:T(1,128)S(1)}) custom-call(f32[20,90,128]{2,1,0:T(8,128)} %state_hbm.1, f32[20,90,128]{2,1,0:T(8,128)} %cot_hbm.1, s32[20,2,90]{2,1,0:T(2,128)} %bitcast.8, f32[20,90]{1,0:T(8,128)} %center_hbm.1, f32[20,4,90]{2,1,0:T(4,128)} %bitcast.7, f32[1,35]{1,0:T(1,128)} %bitcast.9, ...), custom_call_target="tpu_custom_call" | custom-call | flops 1000000000 | bytes 3000000 | tf_op jit(solution)/shard_map/pallas_call | solution.py:771
  31.5 1.0 %shard_map.141 = (f32[20,90,128]{2,1,0:T(8,128)}, f32[1,35]{1,0:T(1,128)}) custom-call(f32[20,104,128]{2,1,0:T(8,128)S(1)} %get-tuple-element.6.result, f32[1,128]{1,0:T(1,128)S(1)} %get-tuple-element.7.totals), custom_call_target="tpu_custom_call" | custom-call | flops 100000000 | bytes 1000000 | tf_op jit(solution)/shard_map/pallas_call | solution.py:819

commit v3 on v2

--- a/solution.py
+++ b/solution.py
@@ -143,8 +143,6 @@
     pieces,
     hot,
     halves,
-    carried,
-    parts,
     bar0,
     drive,
     picked,
@@ -504,18 +502,19 @@
         [jnp.where(row_lane == FIRST_O + k, 1.0, 0.0).astype(BF16) for k in range(5)], axis=1
     )
     spread = jnp.concatenate([spread, spread], axis=0)
-    for n in range(ROWS_DEV // 2):
+
+    @pl.loop(0, GROUPS)
+    def _(g):
         block = jnp.concatenate(
-            [state[2 * n + r, blocked(jj), :] for r in range(2) for jj in range(BLOCKS)], axis=0
+            [state[GROUP * g + r, blocked(jj), :] for r in range(GROUP) for jj in range(BLOCKS)],
+            axis=0,
         )
-        carried[2 * COLS_PAD * n : 2 * COLS_PAD * (n + 1)] = split(block)
-    for g in range(GROUPS):
-        cells = pl.ds(GROUP_CELLS * g, GROUP_CELLS)
-        wide = dot(carried[cells], spread)
+        wide = dot(split(block), spread)
         for k in range(5):
             part = wide[:, CHANNELS * k : CHANNELS * (k + 1)]
-            weights[k, HALO + GROUP * g : HALO + GROUP * (g + 1)] = part.reshape((GROUP,) + ROW)
-        for i in range(GROUP * g, GROUP * (g + 1)):
+            weights[k, pl.ds(HALO + GROUP * g, GROUP)] = part.reshape((GROUP,) + ROW)
+        for r in range(GROUP):
+            i = GROUP * g + r
             for jj in range(BLOCKS):
                 cells = state[i, blocked(jj), :]
                 v0[HALO + i, jj] = jnp.where(weights[0, HALO + i, jj] > 0, cells, 0.0)
@@ -529,14 +528,16 @@
                 halves[i, jj] = halved
 
     loads[4].wait()
-    for n in range(ROWS_DEV // 2):
+
+    @pl.loop(0, GROUPS)
+    def _(g):
         block = jnp.concatenate(
-            [cot[2 * n + r, blocked(jj), :] for r in range(2) for jj in range(BLOCKS)], axis=0
+            [cot[GROUP * g + r, blocked(jj), :] for r in range(GROUP) for jj in range(BLOCKS)],
+            axis=0,
         )
-        parts[2 * COLS_PAD * n : 2 * COLS_PAD * (n + 1)] = split(block)
-    for n in range(GROUPS):
-        cells = pl.ds(GROUP_CELLS * n, GROUP_CELLS)
-        both = dot(parts[cells], maps_twice) + dot(parts[cells, 0:CHANNELS], maps_low)
+        parts = split(block)
+        cells = pl.ds(pl.multiple_of(GROUP_CELLS * g, 8), GROUP_CELLS)
+        both = dot(parts, maps_twice) + dot(parts[:, 0:CHANNELS], maps_low)
         bar0[cells] = both[:, :CHANNELS]
         drive[cells] = both[:, CHANNELS:]
 
@@ -568,14 +569,17 @@
 
     one = (COLS_PAD, CHANNELS)
 
+    def row_cells(r):
+        return pl.ds(COLS_PAD * r if isinstance(r, int) else pl.multiple_of(COLS_PAD * r, 8), COLS_PAD)
+
     def pick_rows(rows):
         moved = [v[SUBSTEPS, HALO + r].reshape(one) * hot[r].reshape(one) for r in rows]
         chosen = dot(split(jnp.concatenate(moved, axis=0)), pick)
         for n, r in enumerate(rows):
-            picked[COLS_PAD * r : COLS_PAD * (r + 1)] = chosen[COLS_PAD * n : COLS_PAD * (n + 1)]
+            picked[row_cells(r)] = chosen[COLS_PAD * n : COLS_PAD * (n + 1)]
 
     def uptake_row(r):
-        cells = slice(COLS_PAD * r, COLS_PAD * (r + 1))
+        cells = row_cells(r)
         p = v[SUBSTEPS, HALO + r].reshape(one)
         halved = halves[r].reshape(one)
         force = drive[cells]
@@ -600,7 +604,6 @@
                 part = pulled[COLS_PAD * n : COLS_PAD * (n + 1)]
                 b[0, HALO + r] += part.reshape(ROW) * hot[r]
 
-    inner_groups = [range(GROUP * g, GROUP * (g + 1)) for g in range(1, GROUPS - 1)]
     outer = list(range(HALO)) + list(range(ROWS_DEV - HALO, ROWS_DEV))
 
     for which in (2, 3):
@@ -610,7 +613,9 @@
         inner_rows(forward_block, v.at[step], v.at[step - 1], step)
     acc[...] = jnp.zeros_like(acc)
 
-    for rows in inner_groups:
+    @pl.loop(1, GROUPS - 1)
+    def _(g):
+        rows = [GROUP * g + r for r in range(GROUP)]
         pick_rows(rows)
         growth_rows(rows, True, False)
 
@@ -674,8 +679,10 @@
     for which in (0, 1, 4, 5, 6, 7):
         send(2, which)
 
-    for rows in inner_groups:
-        growth_rows(rows, False, True)
+    @pl.loop(1, GROUPS - 1)
+    def _(g):
+        growth_rows([GROUP * g + r for r in range(GROUP)], False, True)
+
     b0_cells = b0.reshape(ALL_ROWS * COLS_PAD, CHANNELS)
     for side in range(2):
         cells = []
@@ -788,8 +795,6 @@
             pltpu.VMEM((4, CHANNELS, CHANNELS), F32),
             pltpu.VMEM(cells, F32),
             pltpu.VMEM(cells, F32),
-            pltpu.VMEM((ROWS_DEV * COLS_PAD, 2 * CHANNELS), BF16),
-            pltpu.VMEM((ROWS_DEV * COLS_PAD, 2 * CHANNELS), BF16),
             pltpu.VMEM((ROWS_DEV * COLS_PAD, CHANNELS), F32),
             pltpu.VMEM((ROWS_DEV * COLS_PAD, CHANNELS), F32),
             pltpu.VMEM((ROWS_DEV * COLS_PAD, CHANNELS), F32),

time: 32.6 us -> 32.5 us (level)
  no operation moved by 1% of the time
where the time goes in v3:
time: 32.5 us; the launch traced here: 32.4 us
  Pallas kernels  31.7 us (98%)
  between operations  0.64 us (2%)
    pallas_call x1, Pallas kernels, shards(): pl.pallas_call(kernel, out_shape=(pltpu.VMEM(padded, F32), pltpu.VMEM((1,...  30.7 us
    pallas_call x1, Pallas kernels, shards(): pl.pallas_call(finish_kernel, out_shape=(jax.ShapeDtypeStruct((ROWS_DEV,...  0.97 us

profile of v3, /device:TPU:1, one launch (start us, length us, event | category | flops | bytes accessed | tf_op | source)
XLA Modules:
  0.0 32.4 jit_solution(5367426381505419301)
XLA Ops:
  0.6 30.7 %shard_map.140 = (f32[20,104,128]{2,1,0:T(8,128)S(1)}, f32[1,128]{1,0:T(1,128)S(1)}) custom-call(f32[20,90,128]{2,1,0:T(8,128)} %state_hbm.1, f32[20,90,128]{2,1,0:T(8,128)} %cot_hbm.1, s32[20,2,90]{2,1,0:T(2,128)} %bitcast.8, f32[20,90]{1,0:T(8,128)} %center_hbm.1, f32[20,4,90]{2,1,0:T(4,128)} %bitcast.7, f32[1,35]{1,0:T(1,128)} %bitcast.9, ...), custom_call_target="tpu_custom_call" | custom-call | flops 1000000000 | bytes 3000000 | tf_op jit(solution)/shard_map/pallas_call | solution.py:778
  31.4 1.0 %shard_map.141 = (f32[20,90,128]{2,1,0:T(8,128)}, f32[1,35]{1,0:T(1,128)}) custom-call(f32[20,104,128]{2,1,0:T(8,128)S(1)} %get-tuple-element.6.result, f32[1,128]{1,0:T(1,128)S(1)} %get-tuple-element.7.totals), custom_call_target="tpu_custom_call" | custom-call | flops 100000000 | bytes 1000000 | tf_op jit(solution)/shard_map/pallas_call | solution.py:824
